TPU v7x, 128 devices: a whole 4x4x4 slice. The times are simulated.
128 devices in a mesh: group: 4 (over z), expert: 32 (over x, y, core).
Axes of the slice: x: 4, y: 4, z: 4, core: 2. Of those that a mesh axis runs over, the one named last changes fastest.
Arguments:
- quant_rows: bfloat16 [2, 4096, 3584], P(None, ('group', 'expert')), may hold values from -6 to 6
- row_scales: float32 [2, 4096, 28], P(None, ('group', 'expert')), may hold values from 0.25 to 4
- expert_ids: int32 [2, 4096, 8], P(None, ('group', 'expert')), may hold values from 0 to 127, as said below
- gate_weights: float32 [2, 4096, 8], P(None, ('group', 'expert')), may hold values from 0.1 to 1
- w_gate: bfloat16 [128, 3584, 1024], P(('group', 'expert')), may hold values from -0.09375 to 0.09375
- w_up: bfloat16 [128, 3584, 1024], P(('group', 'expert')), may hold values from -0.09375 to 0.09375
- w_down: bfloat16 [128, 1024, 3584], P(('group', 'expert')), may hold values from -0.1875 to 0.1875
Outputs:
- mixed: bfloat16 [2, 4096, 3584], P(None, ('group', 'expert'))
Inputs may be any that keep to these rules, and one draw needn't show every extreme that they name: `expert_ids`: each token names 8 different experts, 4 in each of exactly 2 groups (expert e lies in group e // 32). In an aligned block of 32 rows of one micro-batch (the rows of one device), one group is common to all tokens, every expert of that group is named by exactly 4 tokens, and no expert is named by more than 4.
All inputs are finite; a program needn't handle non-finite values.
Results may differ from a plain program's by a relative error of at most 0.025.
Values may be sent and summed in bfloat16 or wider, within the bound.
No kernel may reach another device: no remote copies, remote signals or barrier semaphores. Data moves between devices by JAX's collectives and lax.ppermute only.
A program may use at most 128 MiB of HBM per device.

v0:
```python
import jax
import jax.numpy as jnp
from jax import lax
from jax.sharding import PartitionSpec as P

TOPK = 8
BLOCK = 128
MB = 2
CAP = 4


def expert_rows(quant, scales, gate_w, up_w, down_w):
    lead = quant.shape[:-1]
    width = quant.shape[-1]
    values = (
        quant.astype(jnp.float32).reshape(lead + (width // BLOCK, BLOCK))
        * scales.astype(jnp.float32)[..., None]
    )
    rows = values.reshape((-1, width)).astype(jnp.bfloat16)
    gate = jnp.dot(rows, gate_w, preferred_element_type=jnp.float32)
    upper = jnp.dot(rows, up_w, preferred_element_type=jnp.float32)
    hidden = (jax.nn.silu(gate) * upper).astype(jnp.bfloat16)
    result = jnp.dot(hidden, down_w, preferred_element_type=jnp.float32).astype(jnp.bfloat16)
    return result.reshape(lead + (width,))


def slot_layout(ids, experts, slots):
    tok_rows = ids.shape[0]
    flat_ids = ids.reshape(-1)
    onehot = (flat_ids[:, None] == jnp.arange(experts, dtype=jnp.int32)[None, :]).astype(jnp.int32)
    before = jnp.cumsum(onehot, axis=0) - onehot
    rank = jnp.sum(before * onehot, axis=1).reshape(tok_rows, TOPK)
    target = ids * CAP + rank
    return target[:, :, None] == jnp.arange(slots, dtype=jnp.int32)[None, None, :]


def shards(quant_rows, row_scales, expert_ids, gate_weights, w_gate, w_up, w_down):
    n_group = lax.axis_size("group")
    n_inner = lax.axis_size("expert")
    experts = n_group * n_inner
    slots = experts * CAP
    width = quant_rows.shape[2]
    n_scales = row_scales.shape[2]
    gate_w = w_gate[0]
    up_w = w_up[0]
    down_w = w_down[0]
    results = []
    for batch in range(MB):
        quant = quant_rows[batch]
        scales = row_scales[batch]
        ids = expert_ids[batch]
        gates = gate_weights[batch]
        placing = slot_layout(ids, experts, slots)
        scatter_rows = jnp.sum(placing.astype(jnp.int32), axis=1)
        send_quant = jnp.einsum(
            "ts,td->sd",
            scatter_rows.astype(jnp.bfloat16),
            quant,
            preferred_element_type=jnp.float32,
        ).astype(jnp.bfloat16)
        send_scales = jnp.einsum(
            "ts,tb->sb", scatter_rows.astype(jnp.float32), scales, precision=lax.Precision.HIGHEST
        )
        got_quant = lax.all_to_all(
            send_quant.reshape(experts, CAP, width),
            ("group", "expert"),
            split_axis=0,
            concat_axis=0,
            tiled=True,
        )
        got_scales = lax.all_to_all(
            send_scales.reshape(experts, CAP, n_scales).astype(jnp.bfloat16),
            ("group", "expert"),
            split_axis=0,
            concat_axis=0,
            tiled=True,
        ).astype(jnp.float32)
        answer = expert_rows(got_quant, got_scales, gate_w, up_w, down_w)
        back = lax.all_to_all(answer, ("group", "expert"), split_axis=0, concat_axis=0, tiled=True)
        back = back.reshape(slots, width)
        chosen = jnp.einsum(
            "tks,sd->tkd", placing.astype(jnp.bfloat16), back, preferred_element_type=jnp.float32
        )
        total = jnp.sum(gates[:, :, None] * chosen, axis=1)
        results.append(total.astype(jnp.bfloat16))
    return jnp.stack(results, axis=0)


def solution(mesh):
    in_specs = (
        P(None, ("group", "expert"), None),
        P(None, ("group", "expert"), None),
        P(None, ("group", "expert"), None),
        P(None, ("group", "expert"), None),
        P(("group", "expert"), None, None),
        P(("group", "expert"), None, None),
        P(("group", "expert"), None, None),
    )
    out_specs = P(None, ("group", "expert"), None)
    return jax.shard_map(shards, mesh=mesh, in_specs=in_specs, out_specs=out_specs, check_vma=False)
```

profile of v0, /device:TPU:1, one launch (start us, length us, event | category | flops | bytes accessed | tf_op | source)
XLA Modules:
  0.0 294.2 jit_solution(7447810639090495373)
XLA Ops:
  0.0 0.8 fusion.53
  0.8 0.1 copy.92
  0.8 0.1 eq.80
  0.9 0.1 eq.76
  1.0 0.1 copy.70
  1.1 0.2 fusion.38
  1.4 0.2 fusion.43
  1.6 0.1 reshape.123
  1.7 0.2 convert_reduce_fusion.1
  2.0 0.1 copy.73
  2.1 0.9 fusion.52
  3.0 0.4 convolution_convert_fusion.3
  3.4 0.8 copy.76
  4.2 11.5 %all-to-all-start.1 = ((bf16[128,4,28]{2,1,0:T(4,128)(2,1)}), bf16[128,4,28]{2,1,0:T(4,128)(2,1)S(1)}, u32[]{:S(2)}, u32[]{:S(2)}) async-start(bf16[128,4,28]{2,1,0:T(4,128)(2,1)} %copy.76), calls=%async_computation.1 | async-start | bytes 262144 | tf_op jit(solution)/shard_map/all_to_all | solution.py:71
  15.7 0.1 copy.94
  15.7 0.1 eq.91
  15.8 0.1 eq.87
  15.9 0.1 copy.82
  16.0 0.2 fusion.39
  16.3 0.2 fusion.41
  16.5 0.1 reshape.128
  16.6 0.2 convert_reduce_fusion
  16.9 0.1 copy.85
  17.0 0.4 convolution_convert_fusion.2
  17.4 0.8 copy.88
  18.2 7.5 %all-to-all-done.1 = bf16[128,4,28]{2,1,0:T(4,128)(2,1)S(1)} async-done(((bf16[128,4,28]{2,1,0:T(4,128)(2,1)}), bf16[128,4,28]{2,1,0:T(4,128)(2,1)S(1)}, u32[]{:S(2)}, u32[]{:S(2)}) %all-to-all-start.1) | async-done | bytes 28704 | tf_op jit(solution)/shard_map/all_to_all | solution.py:71
  25.7 4.1 %all-to-all-start.4 = ((bf16[128,4,28]{2,1,0:T(4,128)(2,1)}), bf16[128,4,28]{2,1,0:T(4,128)(2,1)S(1)}, u32[]{:S(2)}, u32[]{:S(2)}) async-start(bf16[128,4,28]{2,1,0:T(4,128)(2,1)} %copy.88), calls=%async_computation.4 | async-start | bytes 262144 | tf_op jit(solution)/shard_map/all_to_all | solution.py:71
  29.8 0.0 copy-done
  29.8 2.9 convolution_convert_fusion.1
  32.7 7.0 %reshape.124 = bf16[128,4,3584]{2,1,0:T(4,128)(2,1)} reshape(bf16[512,3584]{1,0:T(8,128)(2,1)} %convolution_convert_fusion.1) | data formatting | bytes 7340032 | tf_op jit(solution)/shard_map/reshape | solution.py:65
  39.8 0.1 all-to-all-done.4
  39.8 10.1 %all-to-all-start = ((bf16[128,4,3584]{2,1,0:T(4,128)(2,1)}), bf16[128,4,3584]{2,1,0:T(4,128)(2,1)}, u32[]{:S(2)}, u32[]{:S(2)}) async-start(bf16[128,4,3584]{2,1,0:T(4,128)(2,1)} %reshape.124), calls=%async_computation | async-start | bytes 7340032 | tf_op jit(solution)/shard_map/all_to_all | solution.py:64
  49.9 3.1 %convolution_convert_fusion = bf16[512,3584]{1,0:T(8,128)(2,1)} fusion(bf16[2,32,3584]{2,1,0:T(8,128)(2,1)S(1)} %copy-done, s32[32,512]{1,0:T(8,128)S(1)} %convert_reduce_fusion), kind=kOutput, calls=%fused_computation.18 | convolution fusion | flops 119291904 | bytes 3964928 | tf_op jit(solution)/shard_map/ts,td->sd/dot_general | solution.py:55
  53.0 7.0 %reshape.129 = bf16[128,4,3584]{2,1,0:T(4,128)(2,1)} reshape(bf16[512,3584]{1,0:T(8,128)(2,1)} %convolution_convert_fusion) | data formatting | bytes 7340032 | tf_op jit(solution)/shard_map/reshape | solution.py:65
  60.0 37.2 %all-to-all-done = bf16[128,4,3584]{2,1,0:T(4,128)(2,1)} async-done(((bf16[128,4,3584]{2,1,0:T(4,128)(2,1)}), bf16[128,4,3584]{2,1,0:T(4,128)(2,1)}, u32[]{:S(2)}, u32[]{:S(2)}) %all-to-all-start) | async-done | bytes 3670048 | tf_op jit(solution)/shard_map/all_to_all | solution.py:64
  97.2 5.3 %all-to-all-start.3 = ((bf16[128,4,3584]{2,1,0:T(4,128)(2,1)}), bf16[128,4,3584]{2,1,0:T(4,128)(2,1)}, u32[]{:S(2)}, u32[]{:S(2)}) async-start(bf16[128,4,3584]{2,1,0:T(4,128)(2,1)} %reshape.129), calls=%async_computation.3 | async-start | bytes 7340032 | tf_op jit(solution)/shard_map/all_to_all | solution.py:64
  102.5 0.1 copy.77
  102.7 7.2 %copy.72 = bf16[128,4,3584]{0,2,1:T(8,128)(2,1)} copy(bf16[128,4,3584]{2,1,0:T(4,128)(2,1)} %all-to-all-done) | data formatting | bytes 7340032 | tf_op jit(solution)/shard_map/all_to_all | solution.py:64
  109.9 4.7 %fusion.13 = bf16[128,4,3584]{0,2,1:T(8,128)(2,1)} fusion(bf16[128,4,3584]{0,2,1:T(8,128)(2,1)} %copy.72, f32[128,4,28]{0,2,1:T(8,128)S(1)} %copy.78), kind=kLoop, calls=%fused_computation.15 | loop fusion | flops 5505024 | bytes 7397376 | tf_op jit(solution)/shard_map/convert_element_type | solution.py:19
  114.5 7.3 %copy.79 = bf16[128,4,3584]{2,1,0:T(4,128)(2,1)} copy(bf16[128,4,3584]{0,2,1:T(8,128)(2,1)} %fusion.13) | data formatting | bytes 7340032 | tf_op jit(solution)/shard_map/convert_element_type | solution.py:19
  121.9 6.7 %convert_element_type.129 = bf16[512,3584]{1,0:T(8,128)(2,1)} reshape(bf16[128,4,3584]{2,1,0:T(4,128)(2,1)} %copy.79) | data formatting | bytes 7340032 | tf_op jit(solution)/shard_map/convert_element_type | solution.py:19
  128.6 7.3 %fusion.7 = f32[512,1024]{1,0:T(8,128)S(1)} fusion(bf16[512,3584]{1,0:T(8,128)(2,1)} %convert_element_type.129, bf16[1,3584,1024]{2,1,0:T(8,128)(2,1)} %param.12), kind=kOutput, calls=%fused_computation.8 | convolution fusion | flops 3758096384 | bytes 13107200 | tf_op jit(solution)/shard_map/dot_general | solution.py:21
  135.9 16.1 %fusion.14 = bf16[512,3584]{1,0:T(8,128)(2,1)} fusion(bf16[1,1024,3584]{2,1,0:T(8,128)(2,1)} %param.13, f32[512,1024]{1,0:T(8,128)S(1)} %fusion.7, bf16[512,3584]{1,0:T(8,128)(2,1)} %convert_element_type.129, bf16[1,3584,1024]{2,1,0:T(8,128)(2,1)} %param.11), kind=kOutput, calls=%fused_computation.16 | convolution fusion | flops 7521173504 | bytes 24117248 | tf_op jit(solution)/shard_map/dot_general | solution.py:23
  152.0 7.0 %reshape.125 = bf16[128,4,3584]{2,1,0:T(4,128)(2,1)} reshape(bf16[512,3584]{1,0:T(8,128)(2,1)} %fusion.14) | data formatting | bytes 7340032 | tf_op jit(solution)/shard_map/reshape | solution.py:24
  159.0 0.0 all-to-all-done.3
  159.1 10.3 %all-to-all-start.2 = ((bf16[128,4,3584]{2,1,0:T(4,128)(2,1)}), bf16[128,4,3584]{2,1,0:T(4,128)(2,1)}, u32[]{:S(2)}, u32[]{:S(2)}) async-start(bf16[128,4,3584]{2,1,0:T(4,128)(2,1)} %reshape.125), calls=%async_computation.2 | async-start | bytes 7340032 | tf_op jit(solution)/shard_map/all_to_all | solution.py:79
  169.4 0.1 copy.89
  169.5 7.2 %copy.84 = bf16[128,4,3584]{0,2,1:T(8,128)(2,1)} copy(bf16[128,4,3584]{2,1,0:T(4,128)(2,1)} %all-to-all-done.3) | data formatting | bytes 7340032 | tf_op jit(solution)/shard_map/all_to_all | solution.py:64
  176.7 4.7 %fusion = bf16[128,4,3584]{0,2,1:T(8,128)(2,1)} fusion(bf16[128,4,3584]{0,2,1:T(8,128)(2,1)} %copy.84, f32[128,4,28]{0,2,1:T(8,128)S(1)} %copy.90), kind=kLoop, calls=%fused_computation.1 | loop fusion | flops 5505024 | bytes 7397376 | tf_op jit(solution)/shard_map/convert_element_type | solution.py:19
  181.4 7.2 %copy.91 = bf16[128,4,3584]{2,1,0:T(4,128)(2,1)} copy(bf16[128,4,3584]{0,2,1:T(8,128)(2,1)} %fusion) | data formatting | bytes 7340032 | tf_op jit(solution)/shard_map/convert_element_type | solution.py:19
  188.6 6.7 %convert_element_type.145 = bf16[512,3584]{1,0:T(8,128)(2,1)} reshape(bf16[128,4,3584]{2,1,0:T(4,128)(2,1)} %copy.91) | data formatting | bytes 7340032 | tf_op jit(solution)/shard_map/convert_element_type | solution.py:19
  195.4 7.3 %fusion.5 = f32[512,1024]{1,0:T(8,128)S(1)} fusion(bf16[512,3584]{1,0:T(8,128)(2,1)} %convert_element_type.145, bf16[1,3584,1024]{2,1,0:T(8,128)(2,1)} %param.12), kind=kOutput, calls=%fused_computation.6 | convolution fusion | flops 3758096384 | bytes 13107200 | tf_op jit(solution)/shard_map/dot_general | solution.py:21
  202.7 16.1 %fusion.17 = bf16[512,3584]{1,0:T(8,128)(2,1)} fusion(bf16[1,1024,3584]{2,1,0:T(8,128)(2,1)} %param.13, f32[512,1024]{1,0:T(8,128)S(1)} %fusion.5, bf16[512,3584]{1,0:T(8,128)(2,1)} %convert_element_type.145, bf16[1,3584,1024]{2,1,0:T(8,128)(2,1)} %param.11), kind=kOutput, calls=%fused_computation.17 | convolution fusion | flops 7521173504 | bytes 24117248 | tf_op jit(solution)/shard_map/dot_general | solution.py:23
  218.8 7.0 %reshape.130 = bf16[128,4,3584]{2,1,0:T(4,128)(2,1)} reshape(bf16[512,3584]{1,0:T(8,128)(2,1)} %fusion.17) | data formatting | bytes 7340032 | tf_op jit(solution)/shard_map/reshape | solution.py:24
  225.8 0.0 all-to-all-done.2
  225.8 10.2 %all-to-all-start.5 = ((bf16[128,4,3584]{2,1,0:T(4,128)(2,1)}), bf16[128,4,3584]{2,1,0:T(4,128)(2,1)}, u32[]{:S(2)}, u32[]{:S(2)}) async-start(bf16[128,4,3584]{2,1,0:T(4,128)(2,1)} %reshape.130), calls=%async_computation.5 | async-start | bytes 7340032 | tf_op jit(solution)/shard_map/all_to_all | solution.py:79
  236.1 0.1 copy.68
  236.1 0.1 copy.80
  236.2 6.7 %reshape.133 = bf16[512,3584,1]{1,0,2:T(8,128)(2,1)} reshape(bf16[128,4,3584]{2,1,0:T(4,128)(2,1)} %all-to-all-done.2) | data formatting | bytes 7340032 | tf_op jit(solution)/shard_map/reshape | solution.py:80
  242.9 3.4 %fusion.24 = bf16[32,3584]{1,0:T(8,128)(2,1)S(1)} fusion(bf16[512,3584,1]{1,0,2:T(8,128)(2,1)} %reshape.133, f32[32,8]{1,0:T(8,128)S(1)} %copy.68, s32[32,8]{1,0:T(8,128)S(1)} %bitcast_add_fusion.1), kind=kOutput, calls=%fused_computation.24 | convolution fusion | flops 941375488 | bytes 3901440 | tf_op jit(solution)/shard_map/tks,sd->tkd/dot_general | solution.py:81
  246.3 36.9 %all-to-all-done.5 = bf16[128,4,3584]{2,1,0:T(4,128)(2,1)} async-done(((bf16[128,4,3584]{2,1,0:T(4,128)(2,1)}), bf16[128,4,3584]{2,1,0:T(4,128)(2,1)}, u32[]{:S(2)}, u32[]{:S(2)}) %all-to-all-start.5) | async-done | bytes 3670048 | tf_op jit(solution)/shard_map/all_to_all | solution.py:79
  283.3 6.7 %reshape.135 = bf16[512,3584,1]{1,0,2:T(8,128)(2,1)} reshape(bf16[128,4,3584]{2,1,0:T(4,128)(2,1)} %all-to-all-done.5) | data formatting | bytes 7340032 | tf_op jit(solution)/shard_map/reshape | solution.py:80
  290.0 3.4 %fusion.25 = bf16[32,3584]{1,0:T(8,128)(2,1)S(1)} fusion(bf16[512,3584,1]{1,0,2:T(8,128)(2,1)} %reshape.135, f32[32,8]{1,0:T(8,128)S(1)} %copy.80, s32[32,8]{1,0:T(8,128)S(1)} %bitcast_add_fusion), kind=kOutput, calls=%fused_computation.25 | convolution fusion | flops 941375488 | bytes 3901440 | tf_op jit(solution)/shard_map/tks,sd->tkd/dot_general | solution.py:81
  293.4 0.8 pad_maximum_fusion
  (22 shorter events, 0.2 us)
Async XLA Ops:
  0.0 29.8 %copy-start = (bf16[2,32,3584]{2,1,0:T(8,128)(2,1)S(1)}, bf16[2,32,3584]{2,1,0:T(8,128)(2,1)}, u32[]{:S(2)}) copy-start(bf16[2,32,3584]{2,1,0:T(8,128)(2,1)} %param.7) | copy-start | bytes 1376260
  4.2 21.5 %all-to-all-start.1 = ((bf16[128,4,28]{2,1,0:T(4,128)(2,1)}), bf16[128,4,28]{2,1,0:T(4,128)(2,1)S(1)}, u32[]{:S(2)}, u32[]{:S(2)}) async-start(bf16[128,4,28]{2,1,0:T(4,128)(2,1)} %copy.76), calls=%async_computation.1 | async-start | bytes 262144 | tf_op jit(solution)/shard_map/all_to_all | solution.py:71
  25.7 14.1 %all-to-all-start.4 = ((bf16[128,4,28]{2,1,0:T(4,128)(2,1)}), bf16[128,4,28]{2,1,0:T(4,128)(2,1)S(1)}, u32[]{:S(2)}, u32[]{:S(2)}) async-start(bf16[128,4,28]{2,1,0:T(4,128)(2,1)} %copy.88), calls=%async_computation.4 | async-start | bytes 262144 | tf_op jit(solution)/shard_map/all_to_all | solution.py:71
  39.8 57.4 %all-to-all-start = ((bf16[128,4,3584]{2,1,0:T(4,128)(2,1)}), bf16[128,4,3584]{2,1,0:T(4,128)(2,1)}, u32[]{:S(2)}, u32[]{:S(2)}) async-start(bf16[128,4,3584]{2,1,0:T(4,128)(2,1)} %reshape.124), calls=%async_computation | async-start | bytes 7340032 | tf_op jit(solution)/shard_map/all_to_all | solution.py:64
  97.2 61.9 %all-to-all-start.3 = ((bf16[128,4,3584]{2,1,0:T(4,128)(2,1)}), bf16[128,4,3584]{2,1,0:T(4,128)(2,1)}, u32[]{:S(2)}, u32[]{:S(2)}) async-start(bf16[128,4,3584]{2,1,0:T(4,128)(2,1)} %reshape.129), calls=%async_computation.3 | async-start | bytes 7340032 | tf_op jit(solution)/shard_map/all_to_all | solution.py:64
  159.1 66.8 %all-to-all-start.2 = ((bf16[128,4,3584]{2,1,0:T(4,128)(2,1)}), bf16[128,4,3584]{2,1,0:T(4,128)(2,1)}, u32[]{:S(2)}, u32[]{:S(2)}) async-start(bf16[128,4,3584]{2,1,0:T(4,128)(2,1)} %reshape.125), calls=%async_computation.2 | async-start | bytes 7340032 | tf_op jit(solution)/shard_map/all_to_all | solution.py:79
  225.8 10.2 %copy-start.1 = (f32[2,32,8]{1,2,0:T(8,128)S(1)}, f32[2,32,8]{1,2,0:T(8,128)}, u32[]{:S(2)}) copy-start(f32[2,32,8]{1,2,0:T(8,128)} %param.10) | copy-start | bytes 6148
  225.8 57.4 %all-to-all-start.5 = ((bf16[128,4,3584]{2,1,0:T(4,128)(2,1)}), bf16[128,4,3584]{2,1,0:T(4,128)(2,1)}, u32[]{:S(2)}, u32[]{:S(2)}) async-start(bf16[128,4,3584]{2,1,0:T(4,128)(2,1)} %reshape.130), calls=%async_computation.5 | async-start | bytes 7340032 | tf_op jit(solution)/shard_map/all_to_all | solution.py:79
where the time goes:
time: 297 us; the launch traced here: 294 us
  local copies, waits for them, and re-layouts  88.8 us (30%)
  waiting for transfers between devices  81.7 us (28%)
  matrix products  60.4 us (20%)
  starting transfers between devices  51.5 us (17%)
  other arithmetic  11.5 us (4%)
    all_to_all x2, waiting for transfers between devices, shards(): lax.all_to_all(send_quant.reshape(experts, CAP, width), ('group', 'expert...  37.2 us
    all_to_all x2, waiting for transfers between devices, shards(): lax.all_to_all(answer, ('group', 'expert'), split_axis=0, concat_axis=0,...  36.9 us
    dot_general x2, matrix products, expert_rows(): jnp.dot(hidden, down_w, preferred_element_type=jnp.float32)  32.3 us
    convert_element_type x4, local copies, waits for them, and re-layouts, expert_rows(): rows = values.reshape((-1, width)).astype(jnp.bfloat16)  28.1 us
    all_to_all x2, starting transfers between devices, shards(): lax.all_to_all(answer, ('group', 'expert'), split_axis=0, concat_axis=0,...  20.5 us
    all_to_all x2, starting transfers between devices, shards(): lax.all_to_all(send_scales.reshape(experts, CAP, n_scales).astype(jnp.bfl...  15.6 us
    all_to_all x2, starting transfers between devices, shards(): lax.all_to_all(send_quant.reshape(experts, CAP, width), ('group', 'expert...  15.4 us
    dot_general x2, matrix products, expert_rows(): upper = jnp.dot(rows, up_w, preferred_element_type=jnp.float32)  14.6 us
  transfers between devices with their start and end apart: 6, of which 4 were waited for; matrix products, arithmetic and copies ran while one was open for 50% of the time, Pallas kernels for 0%

commit v1 on v0

v1 whole, which is shorter than its diff:
```python
import functools

import jax
import jax.numpy as jnp
from jax import lax
from jax.experimental import pallas as pl
from jax.experimental.pallas import tpu as pltpu
from jax.sharding import PartitionSpec as P

BLOCK = 128
CAP = 4
VMEM_LIMIT = 60 * 1024 * 1024


def place_kernel(quant_ref, scale_ref, ids_ref, gate_ref, send_ref, weight_ref, slot_ref):
    tokens = quant_ref.shape[0] * quant_ref.shape[1]
    slots = slot_ref.shape[0]
    batches, topk, rows = ids_ref.shape

    @pl.when(pl.program_id(0) == 0)
    def _():
        row = lax.broadcasted_iota(jnp.int32, (slots, rows), 0)
        expert = row // (batches * CAP)
        lower = (
            lax.broadcasted_iota(jnp.int32, (rows, rows), 0)
            < lax.broadcasted_iota(jnp.int32, (rows, rows), 1)
        ).astype(jnp.bfloat16)
        placed = []
        weighted = []
        for batch in range(batches):
            named = jnp.zeros((slots, rows), jnp.float32)
            weight = jnp.zeros((slots, rows), jnp.float32)
            for k in range(topk):
                hit = expert == ids_ref[batch, k : k + 1, :]
                named += jnp.where(hit, 1.0, 0.0)
                weight += jnp.where(hit, gate_ref[batch, k : k + 1, :], 0.0)
            rank = jnp.dot(named.astype(jnp.bfloat16), lower, preferred_element_type=jnp.float32)
            wanted = (row % (batches * CAP) - batch * CAP).astype(jnp.float32)
            here = jnp.where(rank == wanted, named, 0.0)
            placed.append(here)
            weighted.append(here * weight)
        slot_ref[...] = jnp.concatenate(placed, axis=1).astype(jnp.bfloat16)
        weight_ref[...] = jnp.concatenate(weighted, axis=1)

    width = quant_ref.shape[2]
    quant = quant_ref[...].reshape(tokens, width)
    scale = scale_ref[...].reshape(tokens, width // BLOCK)
    parts = []
    for block in range(width // BLOCK):
        values = quant[:, block * BLOCK : (block + 1) * BLOCK].astype(jnp.float32)
        parts.append((values * scale[:, block : block + 1]).astype(jnp.bfloat16))
    x = jnp.concatenate(parts, axis=1)
    send_ref[...] = jnp.dot(slot_ref[...], x, preferred_element_type=jnp.float32).astype(jnp.bfloat16)


def place_rows(quant, scales, ids, gates, experts):
    batches, rows, width = quant.shape
    tokens = batches * rows
    slots = experts * batches * CAP
    steps = 4
    step_width = width // steps
    step_blocks = step_width // BLOCK
    scales = scales.reshape(batches, rows, steps, step_blocks).transpose(2, 0, 1, 3)
    return pl.pallas_call(
        place_kernel,
        grid=(steps,),
        in_specs=[
            pl.BlockSpec((batches, rows, step_width), lambda i: (0, 0, i)),
            pl.BlockSpec((None, batches, rows, step_blocks), lambda i: (i, 0, 0, 0)),
            pl.BlockSpec(ids.shape, lambda i: (0, 0, 0)),
            pl.BlockSpec(gates.shape, lambda i: (0, 0, 0)),
        ],
        out_specs=[
            pl.BlockSpec((slots, step_width), lambda i: (0, i)),
            pl.BlockSpec((slots, tokens), lambda i: (0, 0)),
        ],
        out_shape=[
            jax.ShapeDtypeStruct((slots, width), jnp.bfloat16),
            jax.ShapeDtypeStruct((slots, tokens), jnp.float32),
        ],
        scratch_shapes=[pltpu.VMEM((slots, tokens), jnp.bfloat16)],
        compiler_params=pltpu.CompilerParams(vmem_limit_bytes=VMEM_LIMIT),
        cost_estimate=pl.CostEstimate(
            flops=2 * slots * tokens * width, bytes_accessed=2 * slots * width, transcendentals=0
        ),
    )(quant, scales, ids, gates)


ROW_TILE = 256


def expert_kernel(n_hidden, x_ref, gate_ref, up_ref, down_ref, y_ref, hidden_ref):
    step = pl.program_id(0)
    rows = x_ref.shape[0]
    tile = gate_ref.shape[1]

    @pl.when(step < n_hidden)
    def _():
        def body(i, carry):
            at = pl.ds(pl.multiple_of(i * ROW_TILE, ROW_TILE), ROW_TILE)
            x = x_ref[at, :]
            gate = jnp.dot(x, gate_ref[...], preferred_element_type=jnp.float32)
            upper = jnp.dot(x, up_ref[...], preferred_element_type=jnp.float32)
            hidden = gate / (1.0 + jnp.exp(-gate)) * upper
            hidden_ref[step, at, :] = hidden.astype(jnp.bfloat16)
            return carry

        lax.fori_loop(0, rows // ROW_TILE, body, 0)

    @pl.when(step >= n_hidden)
    def _():
        def body(i, carry):
            at = pl.ds(pl.multiple_of(i * ROW_TILE, ROW_TILE), ROW_TILE)
            total = jnp.dot(
                jnp.concatenate([hidden_ref[s, at, :] for s in range(n_hidden)], axis=1),
                down_ref[...],
                preferred_element_type=jnp.float32,
            )
            y_ref[at, :] = total.astype(jnp.bfloat16)
            return carry

        lax.fori_loop(0, rows // ROW_TILE, body, 0)


def expert_rows(x, gate_w, up_w, down_w):
    rows, width = x.shape
    hidden = gate_w.shape[1]
    hidden_tile = 256
    out_tile = 512
    n_hidden = hidden // hidden_tile
    n_out = width // out_tile
    first = lambda i: (0, jnp.minimum(i, n_hidden - 1))
    second = lambda i: (0, jnp.maximum(i - n_hidden, 0))
    return pl.pallas_call(
        functools.partial(expert_kernel, n_hidden),
        grid=(n_hidden + n_out,),
        in_specs=[
            pl.BlockSpec((rows, width), lambda i: (0, 0), pipeline_mode=pl.Buffered(1)),
            pl.BlockSpec((width, hidden_tile), first),
            pl.BlockSpec((width, hidden_tile), first),
            pl.BlockSpec((hidden, out_tile), second),
        ],
        out_specs=pl.BlockSpec((rows, out_tile), second),
        out_shape=jax.ShapeDtypeStruct((rows, width), jnp.bfloat16),
        scratch_shapes=[pltpu.VMEM((n_hidden, rows, hidden_tile), jnp.bfloat16)],
        compiler_params=pltpu.CompilerParams(vmem_limit_bytes=VMEM_LIMIT),
        cost_estimate=pl.CostEstimate(
            flops=6 * rows * width * hidden,
            bytes_accessed=6 * width * hidden + 4 * rows * width,
            transcendentals=rows * hidden,
        ),
    )(x, gate_w, up_w, down_w)


def combine_kernel(weight_ref, y_ref, out_ref):
    weight = weight_ref[...]
    high = weight.astype(jnp.bfloat16)
    low = (weight - high.astype(jnp.float32)).astype(jnp.bfloat16)
    both = jnp.concatenate([high, low], axis=1)
    tokens = weight.shape[1]
    y = y_ref[...]
    total = lax.dot_general(both, y, (((0,), (0,)), ((), ())), preferred_element_type=jnp.float32)
    out_ref[...] = (total[:tokens] + total[tokens:]).astype(jnp.bfloat16)


def combine(weights, y):
    slots, width = y.shape
    tokens = weights.shape[1]
    tile = 512
    return pl.pallas_call(
        combine_kernel,
        grid=(width // tile,),
        in_specs=[
            pl.BlockSpec((slots, tokens), lambda i: (0, 0)),
            pl.BlockSpec((slots, tile), lambda i: (0, i)),
        ],
        out_specs=pl.BlockSpec((tokens, tile), lambda i: (0, i)),
        out_shape=jax.ShapeDtypeStruct((tokens, width), jnp.bfloat16),
        compiler_params=pltpu.CompilerParams(vmem_limit_bytes=VMEM_LIMIT),
        cost_estimate=pl.CostEstimate(
            flops=4 * slots * tokens * width, bytes_accessed=2 * slots * width, transcendentals=0
        ),
    )(weights, y)


def shards(quant_rows, row_scales, expert_ids, gate_weights, w_gate, w_up, w_down):
    axes = ("group", "expert")
    experts = lax.axis_size("group") * lax.axis_size("expert")
    batches, rows, width = quant_rows.shape
    ids = expert_ids.transpose(0, 2, 1)
    gates = gate_weights.transpose(0, 2, 1)
    send, weights = place_rows(quant_rows, row_scales, ids, gates, experts)
    per_expert = batches * CAP
    got = lax.all_to_all(send.reshape(experts, per_expert, width), axes, 0, 0, tiled=True)
    answer = expert_rows(got.reshape(experts * per_expert, width), w_gate[0], w_up[0], w_down[0])
    back = lax.all_to_all(answer.reshape(experts, per_expert, width), axes, 0, 0, tiled=True)
    mixed = combine(weights, back.reshape(experts * per_expert, width))
    return mixed.reshape(batches, rows, width)


def solution(mesh):
    tokens = P(None, ("group", "expert"), None)
    weights = P(("group", "expert"), None, None)
    return jax.shard_map(
        shards,
        mesh=mesh,
        in_specs=(tokens, tokens, tokens, tokens, weights, weights, weights),
        out_specs=tokens,
        check_vma=False,
    )
```

time: 297 us -> 245 us (0.82)
  blocking collectives: 0 us -> 191 us
  local copies, waits for them, and re-layouts: 88.8 us -> 1.53 us
  waiting for transfers between devices: 81.7 us -> 0 us
  matrix products: 60.4 us -> 0 us
  Pallas kernels: 0 us -> 52.5 us
  starting transfers between devices: 51.5 us -> 0 us
  other arithmetic: 11.5 us -> 0 us
    all_to_all x0 -> x2, blocking collectives: none -> 191 us  [the longest x1 98.5 us: shards(): lax.all_to_all(send.reshape(experts, per_expert, width), axes, 0, 0, tile...]
    all_to_all x6 -> x0, waiting for transfers between devices: 81.7 us -> none  [the longest x2 37.2 us: shards(): lax.all_to_all(send_quant.reshape(experts, CAP, width), ('group', 'expert...]
    dot_general x10 -> x0, matrix products: 60.4 us -> none  [the longest x2 32.3 us: expert_rows(): jnp.dot(hidden, down_w, preferred_element_type=jnp.float32)]
    pallas_call x0 -> x3, Pallas kernels: none -> 52.5 us  [the longest x1 37 us: expert_rows(): pl.pallas_call(functools.partial(expert_kernel, n_hidden), grid=(n_hidden...]
    all_to_all x6 -> x0, starting transfers between devices: 51.5 us -> none  [the longest x2 20.5 us: shards(): lax.all_to_all(answer, ('group', 'expert'), split_axis=0, concat_axis=0,...]
    reshape x8 -> x1, local copies, waits for them, and re-layouts: 41.7 us -> 1.53 us  [place_rows(): scales.reshape(batches, rows, steps, step_blocks).transpose(2, 0, 1, 3)]
    convert_element_type x10 -> x0, local copies, waits for them, and re-layouts: 29.9 us -> none  [the longest x4 28.1 us: expert_rows(): rows = values.reshape((-1, width)).astype(jnp.bfloat16)]
    all_to_all x4 -> x0, local copies, waits for them, and re-layouts: 14.7 us -> none  [the longest x2 14.4 us: shards(): lax.all_to_all(send_quant.reshape(experts, CAP, width), ('group', 'expert...]
  transfers between devices with their start and end apart: 6 -> 0, of which waited for: 4 -> 0; matrix products, arithmetic and copies ran while one was open for 50% -> 0% of each run, Pallas kernels for 0% -> 0%
where the time goes in v1:
time: 245 us
  blocking collectives  191 us (78%)
  Pallas kernels  52.5 us (21%)
    all_to_all x1, blocking collectives, shards(): lax.all_to_all(send.reshape(experts, per_expert, width), axes, 0, 0, tile...  98.5 us
    all_to_all x1, blocking collectives, shards(): lax.all_to_all(answer.reshape(experts, per_expert, width), axes, 0, 0, ti...  92.3 us
    pallas_call x1, Pallas kernels, expert_rows(): pl.pallas_call(functools.partial(expert_kernel, n_hidden), grid=(n_hidden...  37 us
    pallas_call x1, Pallas kernels, place_rows(): pl.pallas_call(place_kernel, grid=(steps,), in_specs=[pl.BlockSpec((batch...  7.78 us
    pallas_call x1, Pallas kernels, combine(): pl.pallas_call(combine_kernel, grid=(width // tile,), in_specs=[pl.BlockS...  7.7 us

profile of v1, /device:TPU:1, one launch (start us, length us, event | category | flops | bytes accessed | tf_op | source)
XLA Modules:
  0.0 244.8 jit_solution(9985245047287143024)
XLA Ops:
  0.0 1.5 copy.8
  1.5 7.8 %shard_map.73 = (bf16[1024,3584]{1,0:T(8,128)(2,1)}, f32[1024,64]{1,0:T(8,128)}) custom-call(bf16[2,32,3584]{2,1,0:T(8,128)(2,1)} %quant_ref.1, f32[4,2,32,7]{3,2,1,0:T(8,128)} %bitcast.16, s32[2,8,32]{2,1,0:T(8,128)} %bitcast.21, f32[2,8,32]{2,1,0:T(8,128)} %bitcast.22), custom_call_target="tpu_custom_call" | custom-call | flops 469762048 | bytes 7340032 | tf_op jit(solution)/shard_map/pallas_call | solution.py:64
  9.3 98.5 %all_to_all.10 = bf16[128,8,3584]{2,1,0:T(8,128)(2,1)} all-to-all(bf16[128,8,3584]{2,1,0:T(8,128)(2,1)} %bitcast.13), channel_id=1, replica_groups=mesh['group'=4,'expert'=32] {'group','expert'}, dimensions={0} | all-to-all | bytes 14680064 | tf_op jit(solution)/shard_map/all_to_all | solution.py:194
  107.8 37.0 %shard_map.74 = bf16[1024,3584]{1,0:T(8,128)(2,1)} custom-call(bf16[1024,3584]{1,0:T(8,128)(2,1)} %bitcast.14, bf16[3584,1024]{1,0:T(8,128)(2,1)} %bitcast.18, bf16[3584,1024]{1,0:T(8,128)(2,1)} %bitcast.19, bf16[1024,3584]{1,0:T(8,128)(2,1)} %bitcast.20), custom_call_target="tpu_custom_call" | custom-call | flops 22548578304 | bytes 36700160 | tf_op jit(solution)/shard_map/pallas_call | solution.py:134
  144.8 92.3 %all_to_all.11 = bf16[128,8,3584]{2,1,0:T(8,128)(2,1)} all-to-all(bf16[128,8,3584]{2,1,0:T(8,128)(2,1)} %bitcast.15), channel_id=1, replica_groups=mesh['group'=4,'expert'=32] {'group','expert'}, dimensions={0} | all-to-all | bytes 14680064 | tf_op jit(solution)/shard_map/all_to_all | solution.py:196
  237.1 7.7 %shard_map.75 = bf16[64,3584]{1,0:T(8,128)(2,1)} custom-call(f32[1024,64]{1,0:T(8,128)} %get-tuple-element.7.weight_ref, bf16[1024,3584]{1,0:T(8,128)(2,1)} %bitcast.12), custom_call_target="tpu_custom_call" | custom-call | flops 939524096 | bytes 7340032 | tf_op jit(solution)/shard_map/pallas_call | solution.py:170

commit v2 on v1

v2 whole, which is shorter than its diff:
```python
import functools

import jax
import jax.numpy as jnp
from jax import lax
from jax.experimental import pallas as pl
from jax.experimental.pallas import tpu as pltpu
from jax.sharding import PartitionSpec as P

BLOCK = 128
CAP = 4
ROW_TILE = 512
COLUMN_TILE = 512
HIDDEN_TILE = 256
MIB = 1024 * 1024
ANYWHERE = pl.BlockSpec(memory_space=pl.ANY)
IN_VMEM = pl.BlockSpec(memory_space=pltpu.VMEM)


def slot_matrix(ids, gates, slots, batches):
    topk, rows = ids[0].shape
    row = lax.broadcasted_iota(jnp.int32, (slots, rows), 0)
    expert = row // (batches * CAP)
    lower = (
        lax.broadcasted_iota(jnp.int32, (rows, rows), 0) < lax.broadcasted_iota(jnp.int32, (rows, rows), 1)
    ).astype(jnp.bfloat16)
    placed = []
    weighted = []
    for batch in range(batches):
        named = jnp.zeros((slots, rows), jnp.float32)
        weight = jnp.zeros((slots, rows), jnp.float32)
        for k in range(topk):
            hit = expert == ids[batch][k : k + 1, :]
            named += jnp.where(hit, 1.0, 0.0)
            if gates is not None:
                weight += jnp.where(hit, gates[batch][k : k + 1, :], 0.0)
        rank = jnp.dot(named.astype(jnp.bfloat16), lower, preferred_element_type=jnp.float32)
        wanted = (row % (batches * CAP) - batch * CAP).astype(jnp.float32)
        here = jnp.where(rank == wanted, named, 0.0)
        placed.append(here)
        weighted.append(here * weight)
    return jnp.concatenate(weighted if gates is not None else placed, axis=1)


def place_kernel(quant_hbm, scale_hbm, ids_hbm, send_ref, quant_ref, scale_ref, ids_ref, sems):
    batches, rows, width = quant_ref.shape
    slots = send_ref.shape[0]
    loads = [
        pltpu.make_async_copy(source, target, sems.at[i])
        for i, (source, target) in enumerate(
            ((ids_hbm, ids_ref), (scale_hbm, scale_ref), (quant_hbm, quant_ref))
        )
    ]
    for load in loads:
        load.start()
    loads[0].wait()
    placed = slot_matrix([ids_ref[b] for b in range(batches)], None, slots, batches).astype(jnp.bfloat16)
    loads[1].wait()
    scale = jnp.concatenate([scale_ref[:, b, :].T for b in range(batches)], axis=0)
    loads[2].wait()
    quant = quant_ref[...].reshape(batches * rows, width)
    for start in range(0, width, COLUMN_TILE):
        parts = []
        for block in range(start // BLOCK, (start + COLUMN_TILE) // BLOCK):
            values = quant[:, block * BLOCK : (block + 1) * BLOCK].astype(jnp.float32)
            parts.append((values * scale[:, block : block + 1]).astype(jnp.bfloat16))
        x = jnp.concatenate(parts, axis=1)
        send_ref[:, start : start + COLUMN_TILE] = jnp.dot(
            placed, x, preferred_element_type=jnp.float32
        ).astype(jnp.bfloat16)


def place_rows(quant, scales, ids, experts):
    batches, rows, width = quant.shape
    slots = experts * batches * CAP
    return pl.pallas_call(
        place_kernel,
        in_specs=[ANYWHERE, ANYWHERE, ANYWHERE],
        out_specs=IN_VMEM,
        out_shape=jax.ShapeDtypeStruct((slots, width), jnp.bfloat16),
        scratch_shapes=[
            pltpu.VMEM(quant.shape, quant.dtype),
            pltpu.VMEM(scales.shape, scales.dtype),
            pltpu.VMEM(ids.shape, ids.dtype),
            pltpu.SemaphoreType.DMA((3,)),
        ],
        compiler_params=pltpu.CompilerParams(vmem_limit_bytes=10 * MIB),
        cost_estimate=pl.CostEstimate(
            flops=2 * slots * batches * rows * width, bytes_accessed=2 * slots * width, transcendentals=0
        ),
    )(quant, scales, ids)


def expert_kernel(x_ref, gate_ref, up_ref, down_ref, ids_ref, gates_ref, y_ref, weight_ref, hidden_ref):
    rows, width = x_ref.shape
    batches = ids_ref.shape[0]
    tokens = weight_ref.shape[0] // 2
    weight = slot_matrix(
        [ids_ref[b] for b in range(batches)], [gates_ref[b] for b in range(batches)], weight_ref.shape[1], batches
    ).T
    high = weight.astype(jnp.bfloat16)
    weight_ref[0:tokens, :] = high
    weight_ref[tokens:, :] = (weight - high.astype(jnp.float32)).astype(jnp.bfloat16)
    hidden = hidden_ref.shape[1]
    for r in range(0, rows, ROW_TILE):
        at = slice(r, r + ROW_TILE)
        for c in range(0, hidden, HIDDEN_TILE):
            cols = slice(c, c + HIDDEN_TILE)
            gate = jnp.dot(x_ref[at, :], gate_ref[:, cols], preferred_element_type=jnp.float32)
            upper = jnp.dot(x_ref[at, :], up_ref[:, cols], preferred_element_type=jnp.float32)
            half = 0.5 * gate
            hidden_ref[at, cols] = (half * (1.0 + jnp.tanh(half)) * upper).astype(jnp.bfloat16)
    for r in range(0, rows, ROW_TILE):
        at = slice(r, r + ROW_TILE)
        for c in range(0, width, COLUMN_TILE):
            cols = slice(c, c + COLUMN_TILE)
            y_ref[at, cols] = jnp.dot(
                hidden_ref[at, :], down_ref[:, cols], preferred_element_type=jnp.float32
            ).astype(jnp.bfloat16)


def expert_rows(x, gate_w, up_w, down_w, ids, gates):
    rows, width = x.shape
    hidden = gate_w.shape[1]
    batches, _, tokens = ids.shape
    return pl.pallas_call(
        expert_kernel,
        in_specs=[IN_VMEM] * 6,
        out_specs=[IN_VMEM] * 2,
        out_shape=[
            jax.ShapeDtypeStruct((rows, width), jnp.bfloat16),
            jax.ShapeDtypeStruct((2 * batches * tokens, rows), jnp.bfloat16),
        ],
        scratch_shapes=[pltpu.VMEM((rows, hidden), jnp.bfloat16)],
        compiler_params=pltpu.CompilerParams(vmem_limit_bytes=10 * MIB),
        cost_estimate=pl.CostEstimate(
            flops=6 * rows * width * hidden,
            bytes_accessed=6 * width * hidden + 4 * rows * width,
            transcendentals=rows * hidden,
        ),
    )(x, gate_w, up_w, down_w, ids, gates)


def combine_kernel(weight_ref, y_ref, out_ref):
    tokens = out_ref.shape[0]
    for c in range(0, y_ref.shape[1], COLUMN_TILE):
        cols = slice(c, c + COLUMN_TILE)
        total = jnp.dot(weight_ref[...], y_ref[:, cols], preferred_element_type=jnp.float32)
        out_ref[:, cols] = (total[:tokens] + total[tokens:]).astype(jnp.bfloat16)


def combine(weights, y):
    slots, width = y.shape
    tokens = weights.shape[0] // 2
    return pl.pallas_call(
        combine_kernel,
        in_specs=[IN_VMEM, IN_VMEM],
        out_specs=IN_VMEM,
        out_shape=jax.ShapeDtypeStruct((tokens, width), jnp.bfloat16),
        compiler_params=pltpu.CompilerParams(vmem_limit_bytes=10 * MIB),
        cost_estimate=pl.CostEstimate(
            flops=4 * slots * tokens * width, bytes_accessed=2 * slots * width, transcendentals=0
        ),
    )(weights, y)


def shards(quant_rows, row_scales, expert_ids, gate_weights, w_gate, w_up, w_down):
    axes = ("group", "expert")
    experts = lax.axis_size("group") * lax.axis_size("expert")
    batches, rows, width = quant_rows.shape
    ids = expert_ids.transpose(0, 2, 1)
    gates = gate_weights.transpose(0, 2, 1)
    send = place_rows(quant_rows, row_scales.transpose(2, 0, 1), ids, experts)
    per_expert = batches * CAP
    got = lax.all_to_all(send.reshape(experts, per_expert, width), axes, 0, 0, tiled=True)
    answer, weights = expert_rows(
        got.reshape(experts * per_expert, width), w_gate[0], w_up[0], w_down[0], ids, gates
    )
    back = lax.all_to_all(answer.reshape(experts, per_expert, width), axes, 0, 0, tiled=True)
    mixed = combine(weights, back.reshape(experts * per_expert, width))
    return mixed.reshape(batches, rows, width)


def solution(mesh):
    tokens = P(None, ("group", "expert"), None)
    weights = P(("group", "expert"), None, None)
    return jax.shard_map(
        shards,
        mesh=mesh,
        in_specs=(tokens, tokens, tokens, tokens, weights, weights, weights),
        out_specs=tokens,
        check_vma=False,
    )
```

time: 245 us -> 222 us (0.906)
  Pallas kernels: 52.5 us -> 30.6 us
    pallas_call x3, Pallas kernels: 52.5 us -> 30.6 us  [the longest x1 24.9 us: expert_rows(): pl.pallas_call(expert_kernel, in_specs=[IN_VMEM] * 6, out_specs=[IN_VMEM]...]
    unnamed x0 -> x18, local copies, waits for them, and re-layouts: none -> 2.5 us
where the time goes in v2:
time: 222 us
  blocking collectives  189 us (85%)
  Pallas kernels  30.6 us (14%)
  local copies, waits for them, and re-layouts  2.5 us (1%)
    all_to_all x1, blocking collectives, shards(): lax.all_to_all(send.reshape(experts, per_expert, width), axes, 0, 0, tile...  98.2 us
    all_to_all x1, blocking collectives, shards(): lax.all_to_all(answer.reshape(experts, per_expert, width), axes, 0, 0, ti...  90.6 us
    pallas_call x1, Pallas kernels, expert_rows(): pl.pallas_call(expert_kernel, in_specs=[IN_VMEM] * 6, out_specs=[IN_VMEM]...  24.9 us

profile of v2, /device:TPU:1, one launch (start us, length us, event | category | flops | bytes accessed | tf_op | source)
XLA Modules:
  0.0 221.9 jit_solution(17271196941906226004)
XLA Ops:
  0.0 0.0 copy-start
  0.0 1.0 copy-done
  1.0 0.0 copy-start.1
  1.0 0.7 copy-done.1
  1.8 0.0 copy-start.2
  1.8 0.7 copy-done.2
  2.5 0.0 slice-start
  2.5 0.0 slice-start.2
  2.5 3.8 %shard_map.73 = bf16[1024,3584]{1,0:T(8,128)(2,1)S(1)} custom-call(bf16[2,32,3584]{2,1,0:T(8,128)(2,1)S(1)} %copy-done, f32[28,2,32]{2,1,0:T(2,128)S(1)} %bitcast.15, s32[2,8,32]{2,1,0:T(8,128)S(1)} %bitcast.16), custom_call_target="tpu_custom_call" | custom-call | flops 469762048 | bytes 7340032 | tf_op jit(solution)/shard_map/pallas_call | solution.py:76
  6.2 0.0 slice-start.1
  6.2 0.0 slice-start.3
  6.3 0.0 copy-start.3
  6.3 0.0 copy-start.4
  6.3 98.2 %all_to_all.10 = bf16[128,8,3584]{2,1,0:T(8,128)(2,1)S(1)} all-to-all(bf16[128,8,3584]{2,1,0:T(8,128)(2,1)S(1)} %bitcast.11), channel_id=1, replica_groups=mesh['group'=4,'expert'=32] {'group','expert'}, dimensions={0} | all-to-all | bytes 14680064 | tf_op jit(solution)/shard_map/all_to_all | solution.py:175
  104.4 0.0 slice-done
  104.5 0.0 slice-done.2
  104.5 0.0 slice-done.1
  104.5 0.0 slice-done.3
  104.5 0.0 copy-done.3
  104.5 0.0 copy-done.4
  104.5 24.9 %shard_map.74 = (bf16[1024,3584]{1,0:T(8,128)(2,1)S(1)}, bf16[128,1024]{1,0:T(8,128)(2,1)S(1)}) custom-call(bf16[1024,3584]{1,0:T(8,128)(2,1)S(1)} %bitcast.13, bf16[3584,1024]{1,0:T(8,128)(2,1)S(1)} %bitcast.20, bf16[3584,1024]{1,0:T(8,128)(2,1)S(1)} %bitcast.23, bf16[1024,3584]{1,0:T(8,128)(2,1)S(1)} %bitcast.24, s32[2,8,32]{2,1,0:T(8,128)S(1)} %bitcast.17, ...), custom_call_target="tpu_custom_call" | custom-call | flops 22548578304 | bytes 36700160 | tf_op jit(solution)/shard_map/pallas_call | solution.py:126
  129.4 90.6 %all_to_all.11 = bf16[128,8,3584]{2,1,0:T(8,128)(2,1)S(1)} all-to-all(bf16[128,8,3584]{2,1,0:T(8,128)(2,1)S(1)} %bitcast.14), channel_id=1, replica_groups=mesh['group'=4,'expert'=32] {'group','expert'}, dimensions={0} | all-to-all | bytes 14680064 | tf_op jit(solution)/shard_map/all_to_all | solution.py:179
  220.0 1.9 shard_map.75
  (2 shorter events, 0.0 us)
Async XLA Ops:
  0.0 1.0 copy-start
  1.0 0.7 copy-start.1
  1.8 0.7 copy-start.2
  2.5 102.0 %slice-start = ((s8[7340032]{0:T(1024)(128)(4,1)}), s8[4194304]{0:T(1024)(128)(4,1)S(1)}, s32[]{:S(2)}) async-start(s8[7340032]{0:T(1024)(128)(4,1)} %bitcast.18), calls=%async_computation.2 | async-start | bytes 8388608
  2.5 102.0 %slice-start.2 = ((s8[7340032]{0:T(1024)(128)(4,1)}), s8[4194304]{0:T(1024)(128)(4,1)S(1)}, s32[]{:S(2)}) async-start(s8[7340032]{0:T(1024)(128)(4,1)} %bitcast.21), calls=%async_computation.4 | async-start | bytes 8388608
  6.2 98.2 %slice-start.1 = ((s8[7340032]{0:T(1024)(128)(4,1)}), s8[3145728]{0:T(1024)(128)(4,1)S(1)}, s32[]{:S(2)}) async-start(s8[7340032]{0:T(1024)(128)(4,1)} %bitcast.18), calls=%async_computation.3 | async-start | bytes 6291456
  6.2 98.2 %slice-start.3 = ((s8[7340032]{0:T(1024)(128)(4,1)}), s8[3145728]{0:T(1024)(128)(4,1)S(1)}, s32[]{:S(2)}) async-start(s8[7340032]{0:T(1024)(128)(4,1)} %bitcast.21), calls=%async_computation.5 | async-start | bytes 6291456
  6.3 98.2 %copy-start.3 = (bf16[1,1024,3584]{2,1,0:T(8,128)(2,1)S(1)}, bf16[1,1024,3584]{2,1,0:T(8,128)(2,1)}, u32[]{:S(2)}) copy-start(bf16[1,1024,3584]{2,1,0:T(8,128)(2,1)} %param.13) | copy-start | bytes 22020100
  6.3 98.2 %copy-start.4 = (f32[2,32,8]{1,2,0:T(8,128)S(1)}, f32[2,32,8]{1,2,0:T(8,128)}, u32[]{:S(2)}) copy-start(f32[2,32,8]{1,2,0:T(8,128)} %param.10) | copy-start | bytes 6148

commit v3 on v2

--- a/solution.py
+++ b/solution.py
@@ -12,52 +12,47 @@
 ROW_TILE = 512
 COLUMN_TILE = 512
 HIDDEN_TILE = 256
+WEIGHT_TILE = 128
 MIB = 1024 * 1024
-ANYWHERE = pl.BlockSpec(memory_space=pl.ANY)
 IN_VMEM = pl.BlockSpec(memory_space=pltpu.VMEM)
 
 
-def slot_matrix(ids, gates, slots, batches):
-    topk, rows = ids[0].shape
-    row = lax.broadcasted_iota(jnp.int32, (slots, rows), 0)
-    expert = row // (batches * CAP)
-    lower = (
-        lax.broadcasted_iota(jnp.int32, (rows, rows), 0) < lax.broadcasted_iota(jnp.int32, (rows, rows), 1)
-    ).astype(jnp.bfloat16)
-    placed = []
-    weighted = []
-    for batch in range(batches):
-        named = jnp.zeros((slots, rows), jnp.float32)
-        weight = jnp.zeros((slots, rows), jnp.float32)
-        for k in range(topk):
-            hit = expert == ids[batch][k : k + 1, :]
-            named += jnp.where(hit, 1.0, 0.0)
-            if gates is not None:
-                weight += jnp.where(hit, gates[batch][k : k + 1, :], 0.0)
-        rank = jnp.dot(named.astype(jnp.bfloat16), lower, preferred_element_type=jnp.float32)
-        wanted = (row % (batches * CAP) - batch * CAP).astype(jnp.float32)
-        here = jnp.where(rank == wanted, named, 0.0)
-        placed.append(here)
-        weighted.append(here * weight)
-    return jnp.concatenate(weighted if gates is not None else placed, axis=1)
+def slot_matrix(ids, gates, first, experts, batches):
+    topk, tokens = ids.shape
+    rows = tokens // batches
+    per_expert = batches * CAP
+    expert = lax.broadcasted_iota(jnp.int32, (experts, tokens), 0) + first
+    named = jnp.zeros((experts, tokens), jnp.float32)
+    weight = jnp.zeros((experts, tokens), jnp.float32)
+    for k in range(topk):
+        hit = expert == ids[k : k + 1, :]
+        named += jnp.where(hit, 1.0, 0.0)
+        if gates is not None:
+            weight += jnp.where(hit, gates[k : k + 1, :], 0.0)
+    ahead = lax.broadcasted_iota(jnp.int32, (tokens, tokens), 0)
+    token = lax.broadcasted_iota(jnp.int32, (tokens, tokens), 1)
+    lower = jnp.logical_and(ahead < token, ahead // rows == token // rows)
+    rank = jnp.dot(
+        named.astype(jnp.bfloat16),
+        jnp.where(lower, 1.0, 0.0).astype(jnp.bfloat16),
+        preferred_element_type=jnp.float32,
+    )
+    slot = lax.broadcasted_iota(jnp.int32, (1, per_expert, tokens), 1)
+    slot -= CAP * (lax.broadcasted_iota(jnp.int32, (1, per_expert, tokens), 2) // rows)
+    value = named if gates is None else weight
+    shape = (experts, per_expert, tokens)
+    here = jnp.broadcast_to(rank[:, None, :], shape) == slot.astype(jnp.float32)
+    live = jnp.logical_and(here, jnp.broadcast_to(named[:, None, :], shape) > 0.0)
+    placed = jnp.where(live, jnp.broadcast_to(value[:, None, :], shape), 0.0)
+    return placed.reshape(experts * per_expert, tokens)
 
 
-def place_kernel(quant_hbm, scale_hbm, ids_hbm, send_ref, quant_ref, scale_ref, ids_ref, sems):
+def place_kernel(quant_ref, scale_ref, ids_ref, send_ref):
     batches, rows, width = quant_ref.shape
     slots = send_ref.shape[0]
-    loads = [
-        pltpu.make_async_copy(source, target, sems.at[i])
-        for i, (source, target) in enumerate(
-            ((ids_hbm, ids_ref), (scale_hbm, scale_ref), (quant_hbm, quant_ref))
-        )
-    ]
-    for load in loads:
-        load.start()
-    loads[0].wait()
-    placed = slot_matrix([ids_ref[b] for b in range(batches)], None, slots, batches).astype(jnp.bfloat16)
-    loads[1].wait()
+    ids = jnp.concatenate([ids_ref[b] for b in range(batches)], axis=1)
+    placed = slot_matrix(ids, None, 0, slots // (batches * CAP), batches).astype(jnp.bfloat16)
     scale = jnp.concatenate([scale_ref[:, b, :].T for b in range(batches)], axis=0)
-    loads[2].wait()
     quant = quant_ref[...].reshape(batches * rows, width)
     for start in range(0, width, COLUMN_TILE):
         parts = []
@@ -75,15 +70,9 @@
     slots = experts * batches * CAP
     return pl.pallas_call(
         place_kernel,
-        in_specs=[ANYWHERE, ANYWHERE, ANYWHERE],
+        in_specs=[IN_VMEM, IN_VMEM, IN_VMEM],
         out_specs=IN_VMEM,
         out_shape=jax.ShapeDtypeStruct((slots, width), jnp.bfloat16),
-        scratch_shapes=[
-            pltpu.VMEM(quant.shape, quant.dtype),
-            pltpu.VMEM(scales.shape, scales.dtype),
-            pltpu.VMEM(ids.shape, ids.dtype),
-            pltpu.SemaphoreType.DMA((3,)),
-        ],
         compiler_params=pltpu.CompilerParams(vmem_limit_bytes=10 * MIB),
         cost_estimate=pl.CostEstimate(
             flops=2 * slots * batches * rows * width, bytes_accessed=2 * slots * width, transcendentals=0
@@ -95,12 +84,18 @@
     rows, width = x_ref.shape
     batches = ids_ref.shape[0]
     tokens = weight_ref.shape[0] // 2
-    weight = slot_matrix(
-        [ids_ref[b] for b in range(batches)], [gates_ref[b] for b in range(batches)], weight_ref.shape[1], batches
-    ).T
-    high = weight.astype(jnp.bfloat16)
-    weight_ref[0:tokens, :] = high
-    weight_ref[tokens:, :] = (weight - high.astype(jnp.float32)).astype(jnp.bfloat16)
+    ids = jnp.concatenate([ids_ref[b] for b in range(batches)], axis=1)
+    gates = jnp.concatenate([gates_ref[b] for b in range(batches)], axis=1)
+    per_expert = batches * CAP
+
+    def weigh(first):
+        weight = slot_matrix(ids, gates, first // per_expert, WEIGHT_TILE // per_expert, batches).T
+        high = weight.astype(jnp.bfloat16)
+        at = slice(first, first + WEIGHT_TILE)
+        weight_ref[0:tokens, at] = high
+        weight_ref[tokens:, at] = (weight - high.astype(jnp.float32)).astype(jnp.bfloat16)
+
+    pieces = list(range(0, rows, WEIGHT_TILE))
     hidden = hidden_ref.shape[1]
     for r in range(0, rows, ROW_TILE):
         at = slice(r, r + ROW_TILE)
@@ -117,6 +112,8 @@
             y_ref[at, cols] = jnp.dot(
                 hidden_ref[at, :], down_ref[:, cols], preferred_element_type=jnp.float32
             ).astype(jnp.bfloat16)
+            if pieces:
+                weigh(pieces.pop(0))
 
 
 def expert_rows(x, gate_w, up_w, down_w, ids, gates):

time: 222 us -> 220 us (level)
  Pallas kernels: 30.6 us -> 28 us
where the time goes in v3:
time: 220 us; the launch traced here: 219 us
  blocking collectives  189 us (86%)
  Pallas kernels  28 us (13%)
  local copies, waits for them, and re-layouts  2.5 us (1%)
    all_to_all x1, blocking collectives, shards(): lax.all_to_all(send.reshape(experts, per_expert, width), axes, 0, 0, tile...  98.2 us
    all_to_all x1, blocking collectives, shards(): lax.all_to_all(answer.reshape(experts, per_expert, width), axes, 0, 0, ti...  90.6 us
    pallas_call x1, Pallas kernels, expert_rows(): pl.pallas_call(expert_kernel, in_specs=[IN_VMEM] * 6, out_specs=[IN_VMEM]...  23.7 us

profile of v3, /device:TPU:1, one launch (start us, length us, event | category | flops | bytes accessed | tf_op | source)
XLA Modules:
  0.0 219.3 jit_solution(17316600057665153269)
XLA Ops:
  0.0 0.0 copy-start
  0.0 1.0 copy-done
  1.0 0.0 copy-start.1
  1.0 0.7 copy-done.1
  1.8 0.0 copy-start.2
  1.8 0.7 copy-done.2
  2.5 0.0 slice-start
  2.5 0.0 slice-start.2
  2.5 2.4 %shard_map.73 = bf16[1024,3584]{1,0:T(8,128)(2,1)S(1)} custom-call(bf16[2,32,3584]{2,1,0:T(8,128)(2,1)S(1)} %copy-done, f32[28,2,32]{2,1,0:T(2,128)S(1)} %bitcast.15, s32[2,8,32]{2,1,0:T(8,128)S(1)} %bitcast.16), custom_call_target="tpu_custom_call" | custom-call | flops 469762048 | bytes 7340032 | tf_op jit(solution)/shard_map/pallas_call | solution.py:71
  4.8 0.0 slice-start.1
  4.8 0.0 slice-start.3
  4.9 0.0 copy-start.3
  4.9 0.0 copy-start.4
  4.9 98.2 %all_to_all.10 = bf16[128,8,3584]{2,1,0:T(8,128)(2,1)S(1)} all-to-all(bf16[128,8,3584]{2,1,0:T(8,128)(2,1)S(1)} %bitcast.11), channel_id=1, replica_groups=mesh['group'=4,'expert'=32] {'group','expert'}, dimensions={0} | all-to-all | bytes 14680064 | tf_op jit(solution)/shard_map/all_to_all | solution.py:172
  103.0 0.0 slice-done
  103.0 0.0 slice-done.2
  103.0 0.0 slice-done.1
  103.1 0.0 slice-done.3
  103.1 0.0 copy-done.3
  103.1 0.0 copy-done.4
  103.1 23.7 %shard_map.74 = (bf16[1024,3584]{1,0:T(8,128)(2,1)S(1)}, bf16[128,1024]{1,0:T(8,128)(2,1)S(1)}) custom-call(bf16[1024,3584]{1,0:T(8,128)(2,1)S(1)} %bitcast.13, bf16[3584,1024]{1,0:T(8,128)(2,1)S(1)} %bitcast.20, bf16[3584,1024]{1,0:T(8,128)(2,1)S(1)} %bitcast.23, bf16[1024,3584]{1,0:T(8,128)(2,1)S(1)} %bitcast.24, s32[2,8,32]{2,1,0:T(8,128)S(1)} %bitcast.17, ...), custom_call_target="tpu_custom_call" | custom-call | flops 22548578304 | bytes 36700160 | tf_op jit(solution)/shard_map/pallas_call | solution.py:123
  126.8 90.6 %all_to_all.11 = bf16[128,8,3584]{2,1,0:T(8,128)(2,1)S(1)} all-to-all(bf16[128,8,3584]{2,1,0:T(8,128)(2,1)S(1)} %bitcast.14), channel_id=1, replica_groups=mesh['group'=4,'expert'=32] {'group','expert'}, dimensions={0} | all-to-all | bytes 14680064 | tf_op jit(solution)/shard_map/all_to_all | solution.py:176
  217.4 1.9 shard_map.75
  (2 shorter events, 0.0 us)
Async XLA Ops:
  0.0 1.0 copy-start
  1.0 0.7 copy-start.1
  1.8 0.7 copy-start.2
  2.5 100.6 %slice-start = ((s8[7340032]{0:T(1024)(128)(4,1)}), s8[4194304]{0:T(1024)(128)(4,1)S(1)}, s32[]{:S(2)}) async-start(s8[7340032]{0:T(1024)(128)(4,1)} %bitcast.18), calls=%async_computation.2 | async-start | bytes 8388608
  2.5 100.6 %slice-start.2 = ((s8[7340032]{0:T(1024)(128)(4,1)}), s8[4194304]{0:T(1024)(128)(4,1)S(1)}, s32[]{:S(2)}) async-start(s8[7340032]{0:T(1024)(128)(4,1)} %bitcast.21), calls=%async_computation.4 | async-start | bytes 8388608
  4.8 98.2 %slice-start.1 = ((s8[7340032]{0:T(1024)(128)(4,1)}), s8[3145728]{0:T(1024)(128)(4,1)S(1)}, s32[]{:S(2)}) async-start(s8[7340032]{0:T(1024)(128)(4,1)} %bitcast.18), calls=%async_computation.3 | async-start | bytes 6291456
  4.8 98.2 %slice-start.3 = ((s8[7340032]{0:T(1024)(128)(4,1)}), s8[3145728]{0:T(1024)(128)(4,1)S(1)}, s32[]{:S(2)}) async-start(s8[7340032]{0:T(1024)(128)(4,1)} %bitcast.21), calls=%async_computation.5 | async-start | bytes 6291456
  4.9 98.2 %copy-start.3 = (bf16[1,1024,3584]{2,1,0:T(8,128)(2,1)S(1)}, bf16[1,1024,3584]{2,1,0:T(8,128)(2,1)}, u32[]{:S(2)}) copy-start(bf16[1,1024,3584]{2,1,0:T(8,128)(2,1)} %param.13) | copy-start | bytes 22020100
  4.9 98.2 %copy-start.4 = (f32[2,32,8]{1,2,0:T(8,128)S(1)}, f32[2,32,8]{1,2,0:T(8,128)}, u32[]{:S(2)}) copy-start(f32[2,32,8]{1,2,0:T(8,128)} %param.10) | copy-start | bytes 6148

commit v4 on v3

--- a/solution.py
+++ b/solution.py
@@ -14,6 +14,7 @@
 HIDDEN_TILE = 256
 WEIGHT_TILE = 128
 MIB = 1024 * 1024
+ROUTE_VMEM = 53 * MIB
 IN_VMEM = pl.BlockSpec(memory_space=pltpu.VMEM)
 
 
@@ -47,37 +48,75 @@
     return placed.reshape(experts * per_expert, tokens)
 
 
-def place_kernel(quant_ref, scale_ref, ids_ref, send_ref):
+def route_kernel(quant_hbm, scale_hbm, ids_hbm, x_ref, placed_ref, quant_ref, scale_ref, ids_ref, sems):
     batches, rows, width = quant_ref.shape
-    slots = send_ref.shape[0]
+    loads = [
+        pltpu.make_async_copy(source, target, sems.at[i])
+        for i, (source, target) in enumerate(
+            ((ids_hbm, ids_ref), (scale_hbm, scale_ref), (quant_hbm, quant_ref))
+        )
+    ]
+    for load in loads:
+        load.start()
+    loads[0].wait()
     ids = jnp.concatenate([ids_ref[b] for b in range(batches)], axis=1)
-    placed = slot_matrix(ids, None, 0, slots // (batches * CAP), batches).astype(jnp.bfloat16)
+    experts = placed_ref.shape[0] // (batches * CAP)
+    placed_ref[...] = slot_matrix(ids, None, 0, experts, batches).astype(jnp.bfloat16)
+    loads[1].wait()
     scale = jnp.concatenate([scale_ref[:, b, :].T for b in range(batches)], axis=0)
+    loads[2].wait()
     quant = quant_ref[...].reshape(batches * rows, width)
-    for start in range(0, width, COLUMN_TILE):
-        parts = []
-        for block in range(start // BLOCK, (start + COLUMN_TILE) // BLOCK):
-            values = quant[:, block * BLOCK : (block + 1) * BLOCK].astype(jnp.float32)
-            parts.append((values * scale[:, block : block + 1]).astype(jnp.bfloat16))
-        x = jnp.concatenate(parts, axis=1)
-        send_ref[:, start : start + COLUMN_TILE] = jnp.dot(
-            placed, x, preferred_element_type=jnp.float32
-        ).astype(jnp.bfloat16)
-
-
-def place_rows(quant, scales, ids, experts):
+    for block in range(width // BLOCK):
+        cols = slice(block * BLOCK, (block + 1) * BLOCK)
+        x_ref[:, cols] = (quant[:, cols].astype(jnp.float32) * scale[:, block : block + 1]).astype(jnp.bfloat16)
+
+
+def route(quant, scales, ids, experts):
     batches, rows, width = quant.shape
     slots = experts * batches * CAP
+    anywhere = pl.BlockSpec(memory_space=pl.ANY)
+    return pl.pallas_call(
+        route_kernel,
+        in_specs=[anywhere] * 3,
+        out_specs=[IN_VMEM] * 2,
+        out_shape=[
+            jax.ShapeDtypeStruct((batches * rows, width), jnp.bfloat16),
+            jax.ShapeDtypeStruct((slots, batches * rows), jnp.bfloat16),
+        ],
+        scratch_shapes=[
+            pltpu.VMEM(quant.shape, quant.dtype),
+            pltpu.VMEM(scales.shape, scales.dtype),
+            pltpu.VMEM(ids.shape, ids.dtype),
+            pltpu.SemaphoreType.DMA((3,)),
+        ],
+        compiler_params=pltpu.CompilerParams(vmem_limit_bytes=ROUTE_VMEM),
+        cost_estimate=pl.CostEstimate(
+            flops=8 * slots * batches * rows, bytes_accessed=4 * batches * rows * width, transcendentals=0
+        ),
+    )(quant, scales, ids)
+
+
+def place_kernel(placed_ref, x_ref, send_ref):
+    for start in range(0, x_ref.shape[1], COLUMN_TILE):
+        cols = slice(start, start + COLUMN_TILE)
+        send_ref[:, cols] = jnp.dot(
+            placed_ref[...], x_ref[:, cols], preferred_element_type=jnp.float32
+        ).astype(jnp.bfloat16)
+
+
+def place_rows(placed, x):
+    tokens, width = x.shape
+    slots = placed.shape[0]
     return pl.pallas_call(
         place_kernel,
-        in_specs=[IN_VMEM, IN_VMEM, IN_VMEM],
+        in_specs=[IN_VMEM] * 2,
         out_specs=IN_VMEM,
         out_shape=jax.ShapeDtypeStruct((slots, width), jnp.bfloat16),
         compiler_params=pltpu.CompilerParams(vmem_limit_bytes=10 * MIB),
         cost_estimate=pl.CostEstimate(
-            flops=2 * slots * batches * rows * width, bytes_accessed=2 * slots * width, transcendentals=0
-        ),
-    )(quant, scales, ids)
+            flops=2 * slots * tokens * width, bytes_accessed=2 * slots * width, transcendentals=0
+        ),
+    )(placed, x)
 
 
 def expert_kernel(x_ref, gate_ref, up_ref, down_ref, ids_ref, gates_ref, y_ref, weight_ref, hidden_ref):
@@ -167,7 +206,8 @@
     batches, rows, width = quant_rows.shape
     ids = expert_ids.transpose(0, 2, 1)
     gates = gate_weights.transpose(0, 2, 1)
-    send = place_rows(quant_rows, row_scales.transpose(2, 0, 1), ids, experts)
+    x, placed = route(quant_rows, row_scales.transpose(2, 0, 1), ids, experts)
+    send = place_rows(placed, x)
     per_expert = batches * CAP
     got = lax.all_to_all(send.reshape(experts, per_expert, width), axes, 0, 0, tiled=True)
     answer, weights = expert_rows(

time: 220 us -> 219 us (level)
  no operation moved by 1% of the time
where the time goes in v4:
time: 219 us
  blocking collectives  189 us (86%)
  Pallas kernels  28.8 us (13%)
    all_to_all x1, blocking collectives, shards(): lax.all_to_all(send.reshape(experts, per_expert, width), axes, 0, 0, tile...  98.2 us
    all_to_all x1, blocking collectives, shards(): lax.all_to_all(answer.reshape(experts, per_expert, width), axes, 0, 0, ti...  90.6 us
    pallas_call x1, Pallas kernels, expert_rows(): pl.pallas_call(expert_kernel, in_specs=[IN_VMEM] * 6, out_specs=[IN_VMEM]...  23.4 us

profile of v4, /device:TPU:1, one launch (start us, length us, event | category | flops | bytes accessed | tf_op | source)
XLA Modules:
  0.0 219.2 jit_solution(6105620235471070505)
XLA Ops:
  0.0 0.0 copy-start
  0.0 0.7 copy-done
  0.7 0.0 copy-start.1
  0.8 0.7 copy-done.1
  1.4 1.4 shard_map.73
  2.9 0.0 slice-start
  2.9 0.0 slice-start.2
  2.9 2.0 shard_map.74
  4.9 0.0 slice-start.1
  5.0 0.0 slice-start.3
  5.0 0.0 copy-start.2
  5.0 0.0 copy-start.3
  5.0 98.2 %all_to_all.10 = bf16[128,8,3584]{2,1,0:T(8,128)(2,1)S(1)} all-to-all(bf16[128,8,3584]{2,1,0:T(8,128)(2,1)S(1)} %bitcast.12), channel_id=1, replica_groups=mesh['group'=4,'expert'=32] {'group','expert'}, dimensions={0} | all-to-all | bytes 14680064 | tf_op jit(solution)/shard_map/all_to_all | solution.py:212
  103.2 0.0 slice-done
  103.2 0.0 slice-done.2
  103.2 0.0 slice-done.1
  103.2 0.0 slice-done.3
  103.2 0.0 copy-done.2
  103.2 0.0 copy-done.3
  103.2 23.4 %shard_map.75 = (bf16[1024,3584]{1,0:T(8,128)(2,1)S(1)}, bf16[128,1024]{1,0:T(8,128)(2,1)S(1)}) custom-call(bf16[1024,3584]{1,0:T(8,128)(2,1)S(1)} %bitcast.13, bf16[3584,1024]{1,0:T(8,128)(2,1)S(1)} %bitcast.20, bf16[3584,1024]{1,0:T(8,128)(2,1)S(1)} %bitcast.23, bf16[1024,3584]{1,0:T(8,128)(2,1)S(1)} %bitcast.24, s32[2,8,32]{2,1,0:T(8,128)S(1)} %bitcast.17, ...), custom_call_target="tpu_custom_call" | custom-call | flops 22548578304 | bytes 36700160 | tf_op jit(solution)/shard_map/pallas_call | solution.py:162
  126.7 90.6 %all_to_all.11 = bf16[128,8,3584]{2,1,0:T(8,128)(2,1)S(1)} all-to-all(bf16[128,8,3584]{2,1,0:T(8,128)(2,1)S(1)} %bitcast.14), channel_id=1, replica_groups=mesh['group'=4,'expert'=32] {'group','expert'}, dimensions={0} | all-to-all | bytes 14680064 | tf_op jit(solution)/shard_map/all_to_all | solution.py:216
  217.3 1.9 shard_map.76
  (2 shorter events, 0.0 us)
Async XLA Ops:
  0.0 0.7 copy-start
  0.7 0.7 copy-start.1
  2.9 100.3 %slice-start = ((s8[7340032]{0:T(1024)(128)(4,1)}), s8[3145728]{0:T(1024)(128)(4,1)S(1)}, s32[]{:S(2)}) async-start(s8[7340032]{0:T(1024)(128)(4,1)} %bitcast.18), calls=%async_computation.2 | async-start | bytes 6291456
  2.9 100.3 %slice-start.2 = ((s8[7340032]{0:T(1024)(128)(4,1)}), s8[4194304]{0:T(1024)(128)(4,1)S(1)}, s32[]{:S(2)}) async-start(s8[7340032]{0:T(1024)(128)(4,1)} %bitcast.21), calls=%async_computation.4 | async-start | bytes 8388608
  4.9 98.2 %slice-start.1 = ((s8[7340032]{0:T(1024)(128)(4,1)}), s8[4194304]{0:T(1024)(128)(4,1)S(1)}, s32[]{:S(2)}) async-start(s8[7340032]{0:T(1024)(128)(4,1)} %bitcast.18), calls=%async_computation.3 | async-start | bytes 8388608
  5.0 98.2 %slice-start.3 = ((s8[7340032]{0:T(1024)(128)(4,1)}), s8[3145728]{0:T(1024)(128)(4,1)S(1)}, s32[]{:S(2)}) async-start(s8[7340032]{0:T(1024)(128)(4,1)} %bitcast.21), calls=%async_computation.5 | async-start | bytes 6291456
  5.0 98.2 %copy-start.2 = (bf16[1,1024,3584]{2,1,0:T(8,128)(2,1)S(1)}, bf16[1,1024,3584]{2,1,0:T(8,128)(2,1)}, u32[]{:S(2)}) copy-start(bf16[1,1024,3584]{2,1,0:T(8,128)(2,1)} %param.13) | copy-start | bytes 22020100
  5.0 98.2 %copy-start.3 = (f32[2,32,8]{1,2,0:T(8,128)S(1)}, f32[2,32,8]{1,2,0:T(8,128)}, u32[]{:S(2)}) copy-start(f32[2,32,8]{1,2,0:T(8,128)} %param.10) | copy-start | bytes 6148

commit v5 on v4

--- a/solution.py
+++ b/solution.py
@@ -177,12 +177,18 @@
     )(x, gate_w, up_w, down_w, ids, gates)
 
 
-def combine_kernel(weight_ref, y_ref, out_ref):
-    tokens = out_ref.shape[0]
-    for c in range(0, y_ref.shape[1], COLUMN_TILE):
+def combine_kernel(weight_ref, y_ref, out_hbm, out_ref, sems):
+    tokens, width = out_ref.shape
+    stores = []
+    for c in range(0, width, COLUMN_TILE):
         cols = slice(c, c + COLUMN_TILE)
         total = jnp.dot(weight_ref[...], y_ref[:, cols], preferred_element_type=jnp.float32)
         out_ref[:, cols] = (total[:tokens] + total[tokens:]).astype(jnp.bfloat16)
+        at = pl.ds(c, COLUMN_TILE)
+        stores.append(pltpu.make_async_copy(out_ref.at[:, at], out_hbm.at[:, at], sems.at[c // COLUMN_TILE]))
+        stores[-1].start()
+    for store in stores:
+        store.wait()
 
 
 def combine(weights, y):
@@ -191,8 +197,12 @@
     return pl.pallas_call(
         combine_kernel,
         in_specs=[IN_VMEM, IN_VMEM],
-        out_specs=IN_VMEM,
+        out_specs=pl.BlockSpec(memory_space=pl.ANY),
         out_shape=jax.ShapeDtypeStruct((tokens, width), jnp.bfloat16),
+        scratch_shapes=[
+            pltpu.VMEM((tokens, width), jnp.bfloat16),
+            pltpu.SemaphoreType.DMA((width // COLUMN_TILE,)),
+        ],
         compiler_params=pltpu.CompilerParams(vmem_limit_bytes=10 * MIB),
         cost_estimate=pl.CostEstimate(
             flops=4 * slots * tokens * width, bytes_accessed=2 * slots * width, transcendentals=0

time: 219 us -> 220 us (level)
  no operation moved by 1% of the time
where the time goes in v5:
time: 220 us; the launch traced here: 219 us
  blocking collectives  189 us (86%)
  Pallas kernels  28.7 us (13%)
    all_to_all x1, blocking collectives, shards(): lax.all_to_all(send.reshape(experts, per_expert, width), axes, 0, 0, tile...  98.2 us
    all_to_all x1, blocking collectives, shards(): lax.all_to_all(answer.reshape(experts, per_expert, width), axes, 0, 0, ti...  90.6 us
    pallas_call x1, Pallas kernels, expert_rows(): pl.pallas_call(expert_kernel, in_specs=[IN_VMEM] * 6, out_specs=[IN_VMEM]...  23.4 us

profile of v5, /device:TPU:1, one launch (start us, length us, event | category | flops | bytes accessed | tf_op | source)
XLA Modules:
  0.0 219.3 jit_solution(1448591468855214073)
XLA Ops:
  0.0 0.0 copy-start
  0.0 0.7 copy-done
  0.7 0.0 copy-start.1
  0.8 0.7 copy-done.1
  1.4 1.4 shard_map.73
  2.9 0.0 slice-start
  2.9 0.0 slice-start.2
  2.9 2.0 shard_map.74
  4.9 0.0 slice-start.1
  5.0 0.0 slice-start.3
  5.0 0.0 copy-start.2
  5.0 0.0 copy-start.3
  5.0 98.2 %all_to_all.10 = bf16[128,8,3584]{2,1,0:T(8,128)(2,1)S(1)} all-to-all(bf16[128,8,3584]{2,1,0:T(8,128)(2,1)S(1)} %bitcast.12), channel_id=1, replica_groups=mesh['group'=4,'expert'=32] {'group','expert'}, dimensions={0} | all-to-all | bytes 14680064 | tf_op jit(solution)/shard_map/all_to_all | solution.py:222
  103.2 0.0 slice-done
  103.2 0.0 slice-done.2
  103.2 0.0 slice-done.1
  103.2 0.0 slice-done.3
  103.2 0.0 copy-done.2
  103.2 0.0 copy-done.3
  103.2 23.4 %shard_map.75 = (bf16[1024,3584]{1,0:T(8,128)(2,1)S(1)}, bf16[128,1024]{1,0:T(8,128)(2,1)S(1)}) custom-call(bf16[1024,3584]{1,0:T(8,128)(2,1)S(1)} %bitcast.13, bf16[3584,1024]{1,0:T(8,128)(2,1)S(1)} %bitcast.20, bf16[3584,1024]{1,0:T(8,128)(2,1)S(1)} %bitcast.23, bf16[1024,3584]{1,0:T(8,128)(2,1)S(1)} %bitcast.24, s32[2,8,32]{2,1,0:T(8,128)S(1)} %bitcast.17, ...), custom_call_target="tpu_custom_call" | custom-call | flops 22548578304 | bytes 36700160 | tf_op jit(solution)/shard_map/pallas_call | solution.py:162
  126.7 90.6 %all_to_all.11 = bf16[128,8,3584]{2,1,0:T(8,128)(2,1)S(1)} all-to-all(bf16[128,8,3584]{2,1,0:T(8,128)(2,1)S(1)} %bitcast.14), channel_id=1, replica_groups=mesh['group'=4,'expert'=32] {'group','expert'}, dimensions={0} | all-to-all | bytes 14680064 | tf_op jit(solution)/shard_map/all_to_all | solution.py:226
  217.3 1.8 shard_map.76
  (2 shorter events, 0.0 us)
Async XLA Ops:
  0.0 0.7 copy-start
  0.7 0.7 copy-start.1
  2.9 100.3 %slice-start = ((s8[7340032]{0:T(1024)(128)(4,1)}), s8[3145728]{0:T(1024)(128)(4,1)S(1)}, s32[]{:S(2)}) async-start(s8[7340032]{0:T(1024)(128)(4,1)} %bitcast.18), calls=%async_computation.2 | async-start | bytes 6291456
  2.9 100.3 %slice-start.2 = ((s8[7340032]{0:T(1024)(128)(4,1)}), s8[4194304]{0:T(1024)(128)(4,1)S(1)}, s32[]{:S(2)}) async-start(s8[7340032]{0:T(1024)(128)(4,1)} %bitcast.21), calls=%async_computation.4 | async-start | bytes 8388608
  4.9 98.2 %slice-start.1 = ((s8[7340032]{0:T(1024)(128)(4,1)}), s8[4194304]{0:T(1024)(128)(4,1)S(1)}, s32[]{:S(2)}) async-start(s8[7340032]{0:T(1024)(128)(4,1)} %bitcast.18), calls=%async_computation.3 | async-start | bytes 8388608
  5.0 98.2 %slice-start.3 = ((s8[7340032]{0:T(1024)(128)(4,1)}), s8[3145728]{0:T(1024)(128)(4,1)S(1)}, s32[]{:S(2)}) async-start(s8[7340032]{0:T(1024)(128)(4,1)} %bitcast.21), calls=%async_computation.5 | async-start | bytes 6291456
  5.0 98.2 %copy-start.2 = (bf16[1,1024,3584]{2,1,0:T(8,128)(2,1)S(1)}, bf16[1,1024,3584]{2,1,0:T(8,128)(2,1)}, u32[]{:S(2)}) copy-start(bf16[1,1024,3584]{2,1,0:T(8,128)(2,1)} %param.13) | copy-start | bytes 22020100
  5.0 98.2 %copy-start.3 = (f32[2,32,8]{1,2,0:T(8,128)S(1)}, f32[2,32,8]{1,2,0:T(8,128)}, u32[]{:S(2)}) copy-start(f32[2,32,8]{1,2,0:T(8,128)} %param.10) | copy-start | bytes 6148
